TPU v7x, 32 devices: a whole 2x2x4 slice. The times are simulated.
32 devices in a mesh: tx: 8 (over y, x, core), ty: 4 (over z).
Axes of the slice: x: 2, y: 2, z: 4, core: 2. Of those that a mesh axis runs over, the one named last changes fastest.
Arguments:
- adjoint_in: float32 [5, 3, 64, 64, 128], P(None, None, 'ty', 'tx'), may hold values from -6 to 6
- courant: float32 [2, 3, 64, 64, 128], P(None, None, 'ty', 'tx'), may hold values from -0.45 to 0.45
- vertical_inverse: float32 [5, 128, 128], replicated, as said below
- links: int32 [40, 4], replicated, may hold values from 0 to 95, as said below
Outputs:
- adjoint_out: float32 [5, 3, 64, 64, 128], P(None, None, 'ty', 'tx')
Inputs may be any that keep to these rules, and one draw needn't show every extreme that they name: `links`: the three panel slots hold three faces of a cube that meet at one corner, in an order drawn afresh; call them X, Y, Z. X's east side joins Y's west side (code 0, both ways, tile row to same tile row), X's north side joins Z's south side (code 1, both ways, tile column to same tile column), Y's north side joins Z's east side with rotation: cell x = i of Y's top row is the neighbour of cell y = i of Z's east column (code 2 for Z's east ghosts, two rows a tile with off 0 and 8; code 3 for Y's north ghosts, one row a tile with off 0 or 8); all other panel sides are open. Row order is drawn afresh. Offsets are 0 or 8, codes 0 to 3. `vertical_inverse`: each block has a diagonal in [0.6, 1.0) and independent off-diagonal entries.
All inputs are finite; a program needn't handle non-finite values.
Results may differ from a plain program's by a relative error of at most 0.0003.
Values sent between devices are 32-bit elements; how exact they have to be, the bound alone decides.
A program may use at most 64 MiB of HBM per device.

v0:
```python
import jax
import jax.numpy as jnp
from jax import lax
from jax.sharding import PartitionSpec as P

STEPS = 2


def with_halo(block, sides, width):
    for axis, dim in sides:
        count = lax.axis_size(axis)
        forward = [(i, i + 1) for i in range(count - 1)]
        forward.append((count - 1, 0))
        backward = [(target, source) for source, target in forward]
        low = lax.ppermute(
            lax.slice_in_dim(block, block.shape[dim] - width, None, axis=dim), axis, forward
        )
        high = lax.ppermute(lax.slice_in_dim(block, 0, width, axis=dim), axis, backward)
        block = jnp.concatenate([low, block, high], axis=dim)
    return block


def broadcast(block, axis, source):
    block = jnp.where(lax.axis_index(axis) == source, block, jnp.zeros_like(block))
    return lax.psum(block, axis)


def link_tables(links, own_tile, tile_count, slot_count):
    source_slot = links[:, 0] // tile_count
    target_slot = links[:, 1] // tile_count
    target_tile = links[:, 1] % tile_count
    offset = links[:, 2]
    link_kind = links[:, 3]
    slot_ids = jnp.arange(slot_count, dtype=jnp.int32)
    target_hot = (target_slot[:, None] == slot_ids[None, :]).astype(jnp.float32)
    source_hot = (source_slot[:, None] == slot_ids[None, :]).astype(jnp.float32)

    def slot_table(wanted):
        chosen = (
            (target_tile == own_tile) & (link_kind == wanted) & ((link_kind != 2) | (offset == 0))
        )
        weight = chosen.astype(jnp.float32)
        return jnp.sum(
            weight[:, None, None] * target_hot[:, :, None] * source_hot[:, None, :], axis=0
        )

    north_source = jnp.max(jnp.where(link_kind == 2, source_slot, 0))
    east_source = jnp.max(jnp.where(link_kind == 3, source_slot, 0))
    return (slot_table(0), slot_table(1), slot_table(2), slot_table(3), north_source, east_source)


def mix_slots(slot_table, pieces):
    return jnp.sum(slot_table[None, :, :, None, None] * pieces[:, None], axis=2)


def on_device(adjoint_in, courant, vertical_inverse, links):
    col_count = lax.axis_size("tx")
    row_count = lax.axis_size("ty")
    column = lax.axis_index("tx")
    row_index = lax.axis_index("ty")
    slot_count = adjoint_in.shape[1]
    cells_y = adjoint_in.shape[2]
    cells_x = adjoint_in.shape[3]
    tile_count = col_count * row_count
    own_tile = row_index * col_count + column
    x_table, y_table, east_table, north_table, north_source, east_source = link_tables(
        links, own_tile, tile_count, slot_count
    )
    at_east = column == col_count - 1
    at_west = column == 0
    at_north = row_index == row_count - 1
    at_south = row_index == 0
    adjoint = adjoint_in
    for step_index in range(STEPS):
        mixed = jnp.einsum(
            "slm,skyxl->skyxm", vertical_inverse, adjoint, precision=lax.Precision.HIGHEST
        )
        fluxes = courant[:, None] * mixed[None]
        padded = with_halo(fluxes, (("tx", 4), ("ty", 3)), 1)
        halo_east = padded[0, :, :, 1:-1, cells_x + 1]
        halo_west = padded[0, :, :, 1:-1, 0]
        halo_north = padded[1, :, :, cells_y + 1, 1:-1]
        halo_south = padded[1, :, :, 0, 1:-1]
        top_rows = lax.dynamic_slice_in_dim(fluxes[1, :, :, cells_y - 1], north_source, 1, 1)
        east_cols = lax.dynamic_slice_in_dim(fluxes[0, :, :, :, cells_x - 1], east_source, 1, 1)
        north_below = broadcast(top_rows, "ty", row_count - 1)
        north_whole = lax.all_gather(north_below, "tx", axis=2, tiled=True)
        east_beside = broadcast(east_cols, "tx", col_count - 1)
        east_whole = lax.all_gather(east_beside, "ty", axis=2, tiled=True)
        north_piece = lax.dynamic_slice_in_dim(north_whole, row_index * cells_y, cells_y, 2)
        east_piece = lax.dynamic_slice_in_dim(east_whole, column * cells_x, cells_x, 2)
        rotated_east = -jnp.sum(east_table, axis=1)[None, :, None, None] * north_piece
        rotated_north = -jnp.sum(north_table, axis=1)[None, :, None, None] * east_piece
        ghost_east = jnp.where(at_east, mix_slots(x_table, halo_east) + rotated_east, halo_east)
        ghost_west = jnp.where(at_west, mix_slots(x_table, halo_west), halo_west)
        ghost_north = jnp.where(
            at_north, mix_slots(y_table, halo_north) + rotated_north, halo_north
        )
        ghost_south = jnp.where(at_south, mix_slots(y_table, halo_south), halo_south)
        x_line = jnp.concatenate(
            [ghost_west[:, :, :, None], fluxes[0], ghost_east[:, :, :, None]], axis=3
        )
        y_line = jnp.concatenate(
            [ghost_south[:, :, None], fluxes[1], ghost_north[:, :, None]], axis=2
        )
        adjoint = (
            mixed
            + 0.5 * (x_line[:, :, :, 2:] - x_line[:, :, :, :-2])
            + 0.5 * (y_line[:, :, 2:] - y_line[:, :, :-2])
        )
    return adjoint


def solution(mesh):
    placed = (P(None, None, "ty", "tx", None), P(None, None, "ty", "tx", None), P(), P())
    return jax.shard_map(
        on_device,
        mesh=mesh,
        in_specs=placed,
        out_specs=P(None, None, "ty", "tx", None),
        check_vma=False,
    )
```

profile of v0, /device:TPU:0, one launch (start us, length us, event | category | flops | bytes accessed | tf_op | source)
XLA Modules:
  0.0 178.6 jit_solution(6658720027340490278)
XLA Ops:
  0.0 1.2 copy.186
  1.3 1.9 %fusion.13 = f32[5,3,16,8,128]{4,3,2,1,0:T(8,128)S(1)} fusion(f32[5,3,16,8,128]{4,3,2,1,0:T(8,128)S(1)} %copy-done, f32[5,128,128]{2,1,0:T(8,128)} %param.6), kind=kOutput, calls=%fused_computation.33 | convolution fusion | flops 377487360 | bytes 2293760 | tf_op jit(solution)/shard_map/slm,skyxl->skyxm/dot_general | solution.py:75
  3.3 0.9 copy-done.1
  4.6 0.8 fusion.36
  5.9 2.9 %collective-permute-start = (f32[2,5,3,16,1,128]{5,3,2,1,4,0:T(8,128)}, f32[2,5,3,16,1,128]{5,3,2,1,4,0:T(8,128)}, u32[]{:S(2)}, u32[]{:S(2)}) collective-permute-start(f32[2,5,3,16,1,128]{5,3,2,1,4,0:T(8,128)} %get-tuple-element.33), channel_id=1, source_target_pairs={{4,0},{8,4},{12,8},{16,12},{20,16},{24,20},{28,24},{0,28},{5,1},{9... | collective-permute-start | bytes 737288 | tf_op jit(solution)/shard_map/ppermute | solution.py:18
  8.8 0.7 fusion.28
  12.5 0.6 neg.18
  14.3 20.5 %psum.28 = f32[5,1,8,128]{3,2,0,1:T(8,128)} all-reduce(f32[5,1,8,128]{3,2,0,1:T(8,128)S(1)} %bitcast.157), channel_id=1, replica_groups=mesh['tx'=8,'ty'=4] {'ty'}, use_global_device_ids=true, to_apply=%region_4.5 | all-reduce | flops 5120 | bytes 40960 | tf_op jit(solution)/shard_map/psum | solution.py:25
  35.5 22.7 %psum.29 = f32[5,1,16,128]{3,2,0,1:T(8,128)S(1)} all-reduce(f32[5,1,16,128]{3,2,0,1:T(8,128)S(1)} %select_bitcast_fusion.1), channel_id=1, replica_groups=mesh['tx'=8,'ty'=4] {'tx'}, use_global_device_ids=true, to_apply=%region_10.11 | all-reduce | flops 10240 | bytes 81920 | tf_op jit(solution)/shard_map/psum | solution.py:25
  58.3 13.5 %all_gather.13 = f32[5,1,64,128]{3,2,0,1:T(8,128)S(1)} all-gather(f32[5,1,16,128]{3,2,0,1:T(8,128)S(1)} %psum.29), channel_id=1, replica_groups=mesh['tx'=8,'ty'=4] {'ty'}, dimensions={2}, use_global_device_ids=true | all-gather | bytes 204800 | tf_op jit(solution)/shard_map/all_gather | solution.py:89
  71.7 9.5 %all_gather.12 = f32[5,1,64,128]{3,2,0,1:T(8,128)S(1)} all-gather(f32[5,1,8,128]{3,2,0,1:T(8,128)} %psum.28), channel_id=1, replica_groups=mesh['tx'=8,'ty'=4] {'tx'}, dimensions={2}, use_global_device_ids=true | all-gather | bytes 184320 | tf_op jit(solution)/shard_map/all_gather | solution.py:87
  81.4 1.3 pad_maximum_fusion.13
  82.8 1.9 %collective-permute-start.3 = (f32[2,5,3,1,10,128]{5,3,2,1,4,0:T(1,128)S(1)}, f32[2,5,3,1,10,128]{5,3,2,1,4,0:T(1,128)S(1)}, u32[]{:S(2)}, u32[]{:S(2)}) collective-permute-start(f32[2,5,3,1,10,128]{5,3,2,1,4,0:T(1,128)S(1)} %get-tuple-element.25), channel_id=1, source_target_pairs={{0,1},{1,2},{2,3},{3,0},{4,5},{5,6},{6,7},{7,4},{8,9},{9,10},{10,1... | collective-permute-start | bytes 460808 | tf_op jit(solution)/shard_map/ppermute | solution.py:15
  84.8 0.9 slice_bitcast_fusion.4
  85.7 0.9 slice_bitcast_fusion.5
  86.7 1.0 bitcast_select_fusion.2
  87.7 0.9 bitcast_select_fusion.1
  88.8 0.7 collective-permute-done.2
  89.5 2.8 %collective-permute-done.3 = f32[2,5,3,1,10,128]{5,3,2,1,4,0:T(1,128)S(1)} collective-permute-done((f32[2,5,3,1,10,128]{5,3,2,1,4,0:T(1,128)S(1)}, f32[2,5,3,1,10,128]{5,3,2,1,4,0:T(1,128)S(1)}, u32[]{:S(2)}, u32[]{:S(2)}) %collective-permute-start.3) | collective-permute-done | bytes 153632 | tf_op jit(solution)/shard_map/ppermute | solution.py:15
  93.0 1.7 fusion.9
  95.8 0.8 fusion.35
  96.6 1.4 slice_bitcast_fusion
  98.1 23.2 %psum.31 = f32[5,1,16,128]{3,2,0,1:T(8,128)S(1)} all-reduce(f32[5,1,16,128]{3,2,0,1:T(8,128)S(1)} %select_bitcast_fusion), channel_id=1, replica_groups=mesh['tx'=8,'ty'=4] {'tx'}, use_global_device_ids=true, to_apply=%region_16.17 | all-reduce | flops 10240 | bytes 81920 | tf_op jit(solution)/shard_map/psum | solution.py:25
  121.3 13.4 %all_gather.15 = f32[5,1,64,128]{3,2,0,1:T(8,128)S(1)} all-gather(f32[5,1,16,128]{3,2,0,1:T(8,128)S(1)} %psum.31), channel_id=1, replica_groups=mesh['tx'=8,'ty'=4] {'ty'}, dimensions={2}, use_global_device_ids=true | all-gather | bytes 204800 | tf_op jit(solution)/shard_map/all_gather | solution.py:89
  134.7 2.6 %collective-permute-start.4 = (f32[2,5,3,16,1,128]{5,3,2,1,4,0:T(8,128)}, f32[2,5,3,16,1,128]{5,3,2,1,4,0:T(8,128)S(1)}, u32[]{:S(2)}, u32[]{:S(2)}) collective-permute-start(f32[2,5,3,16,1,128]{5,3,2,1,4,0:T(8,128)} %get-tuple-element.29), channel_id=1, source_target_pairs={{4,0},{8,4},{12,8},{16,12},{20,16},{24,20},{28,24},{0,28},{5,1},{9... | collective-permute-start | bytes 737288 | tf_op jit(solution)/shard_map/ppermute | solution.py:18
  137.4 2.5 %copy.252 = f32[1,5,3,16,8,128]{5,4,3,2,1,0:T(8,128)} copy(f32[1,5,3,16,8,128]{5,3,2,1,4,0:T(8,128)} %get-tuple-element.27) | data formatting | bytes 1966080 | tf_op jit(solution)/shard_map/slice | solution.py:101
  139.9 17.6 %psum.30 = f32[5,1,8,128]{3,2,0,1:T(8,128)S(1)} all-reduce(f32[5,1,8,128]{3,2,0,1:T(8,128)S(1)} %bitcast.156), channel_id=1, replica_groups=mesh['tx'=8,'ty'=4] {'ty'}, use_global_device_ids=true, to_apply=%region_13.14 | all-reduce | flops 5120 | bytes 40960 | tf_op jit(solution)/shard_map/psum | solution.py:25
  157.5 8.7 %all_gather.14 = f32[5,1,64,128]{3,2,0,1:T(8,128)S(1)} all-gather(f32[5,1,8,128]{3,2,0,1:T(8,128)S(1)} %psum.30), channel_id=1, replica_groups=mesh['tx'=8,'ty'=4] {'tx'}, dimensions={2}, use_global_device_ids=true | all-gather | bytes 184320 | tf_op jit(solution)/shard_map/all_gather | solution.py:87
  166.5 2.0 %collective-permute-start.7 = (f32[2,5,3,1,10,128]{5,3,2,1,4,0:T(1,128)S(1)}, f32[2,5,3,1,10,128]{5,3,2,1,4,0:T(1,128)S(1)}, u32[]{:S(2)}, u32[]{:S(2)}) collective-permute-start(f32[2,5,3,1,10,128]{5,3,2,1,4,0:T(1,128)S(1)} %get-tuple-element.23), channel_id=1, source_target_pairs={{0,1},{1,2},{2,3},{3,0},{4,5},{5,6},{6,7},{7,4},{8,9},{9,10},{10,1... | collective-permute-start | bytes 460808 | tf_op jit(solution)/shard_map/ppermute | solution.py:15
  168.8 4.4 %collective-permute-done.6 = f32[2,5,3,1,10,128]{5,3,2,1,4,0:T(1,128)S(1)} collective-permute-done((f32[2,5,3,1,10,128]{5,3,2,1,4,0:T(1,128)S(1)}, f32[2,5,3,1,10,128]{5,3,2,1,4,0:T(1,128)S(1)}, u32[]{:S(2)}, u32[]{:S(2)}) %collective-permute-start.6) | collective-permute-done | bytes 153632 | tf_op jit(solution)/shard_map/ppermute | solution.py:18
  173.3 2.8 %collective-permute-done.7 = f32[2,5,3,1,10,128]{5,3,2,1,4,0:T(1,128)S(1)} collective-permute-done((f32[2,5,3,1,10,128]{5,3,2,1,4,0:T(1,128)S(1)}, f32[2,5,3,1,10,128]{5,3,2,1,4,0:T(1,128)S(1)}, u32[]{:S(2)}, u32[]{:S(2)}) %collective-permute-start.7) | collective-permute-done | bytes 153632 | tf_op jit(solution)/shard_map/ppermute | solution.py:15
  176.8 1.8 fusion.4
  (82 shorter events, 5.3 us)
Async XLA Ops:
  0.0 1.3 copy-start
  3.3 0.9 copy-start.1
  4.4 4.3 %copy-start.8 = (s32[40,4]{0,1:T(4,128)S(1)}, s32[40,4]{0,1:T(4,128)}, u32[]{:S(2)}) copy-start(s32[40,4]{0,1:T(4,128)} %param.7) | copy-start | bytes 1924
  5.4 75.9 %collective-permute-start.1 = (f32[2,5,3,16,1,128]{5,3,2,1,4,0:T(8,128)}, f32[2,5,3,16,1,128]{5,3,2,1,4,0:T(8,128)}, u32[]{:S(2)}, u32[]{:S(2)}) collective-permute-start(f32[2,5,3,16,1,128]{5,3,2,1,4,0:T(8,128)} %get-tuple-element.32), channel_id=1, source_target_pairs={{0,4},{4,8},{8,12},{12,16},{16,20},{20,24},{24,28},{28,0},{1,5},{5... | collective-permute-start | bytes 737288 | tf_op jit(solution)/shard_map/ppermute | solution.py:15
  5.9 75.5 %collective-permute-start = (f32[2,5,3,16,1,128]{5,3,2,1,4,0:T(8,128)}, f32[2,5,3,16,1,128]{5,3,2,1,4,0:T(8,128)}, u32[]{:S(2)}, u32[]{:S(2)}) collective-permute-start(f32[2,5,3,16,1,128]{5,3,2,1,4,0:T(8,128)} %get-tuple-element.33), channel_id=1, source_target_pairs={{4,0},{8,4},{12,8},{16,12},{20,16},{24,20},{28,24},{0,28},{5,1},{9... | collective-permute-start | bytes 737288 | tf_op jit(solution)/shard_map/ppermute | solution.py:18
  81.3 5.4 %copy-start.10 = (f32[3]{0:T(128)S(1)}, f32[3]{0:T(128)}, u32[]{:S(2)}) copy-start(f32[3]{0:T(128)} %neg.18) | copy-start | bytes 40
  82.7 6.8 %collective-permute-start.2 = (f32[2,5,3,1,10,128]{5,3,2,1,4,0:T(1,128)S(1)}, f32[2,5,3,1,10,128]{5,3,2,1,4,0:T(1,128)S(1)}, u32[]{:S(2)}, u32[]{:S(2)}) collective-permute-start(f32[2,5,3,1,10,128]{5,3,2,1,4,0:T(1,128)S(1)} %get-tuple-element.24), channel_id=1, source_target_pairs={{1,0},{2,1},{3,2},{0,3},{5,4},{6,5},{7,6},{4,7},{9,8},{10,9},{11,1... | collective-permute-start | bytes 460808 | tf_op jit(solution)/shard_map/ppermute | solution.py:18
  82.8 9.5 %collective-permute-start.3 = (f32[2,5,3,1,10,128]{5,3,2,1,4,0:T(1,128)S(1)}, f32[2,5,3,1,10,128]{5,3,2,1,4,0:T(1,128)S(1)}, u32[]{:S(2)}, u32[]{:S(2)}) collective-permute-start(f32[2,5,3,1,10,128]{5,3,2,1,4,0:T(1,128)S(1)} %get-tuple-element.25), channel_id=1, source_target_pairs={{0,1},{1,2},{2,3},{3,0},{4,5},{5,6},{6,7},{7,4},{8,9},{9,10},{10,1... | collective-permute-start | bytes 460808 | tf_op jit(solution)/shard_map/ppermute | solution.py:15
  86.7 5.9 %copy-start.9 = (f32[3]{0:T(128)S(1)}, f32[3]{0:T(128)}, u32[]{:S(2)}) copy-start(f32[3]{0:T(128)} %neg.19) | copy-start | bytes 40
  88.7 4.3 %copy-start.2 = (f32[5,3,16,8,128]{4,3,2,1,0:T(8,128)S(1)}, f32[5,3,16,8,128]{4,3,2,1,0:T(8,128)}, u32[]{:S(2)}) copy-start(f32[5,3,16,8,128]{4,3,2,1,0:T(8,128)} %copy-done.1) | copy-start | bytes 2949124
  88.8 4.3 %copy-start.7 = (f32[5,128,128]{2,1,0:T(8,128)S(1)}, f32[5,128,128]{2,1,0:T(8,128)}, u32[]{:S(2)}) copy-start(f32[5,128,128]{2,1,0:T(8,128)} %param.6) | copy-start | bytes 983044
  94.8 0.9 copy-start.3
  134.7 31.5 %collective-permute-start.5 = (f32[2,5,3,16,1,128]{5,3,2,1,4,0:T(8,128)}, f32[2,5,3,16,1,128]{5,3,2,1,4,0:T(8,128)S(1)}, u32[]{:S(2)}, u32[]{:S(2)}) collective-permute-start(f32[2,5,3,16,1,128]{5,3,2,1,4,0:T(8,128)} %get-tuple-element.28), channel_id=1, source_target_pairs={{0,4},{4,8},{8,12},{12,16},{16,20},{20,24},{24,28},{28,0},{1,5},{5... | collective-permute-start | bytes 737288 | tf_op jit(solution)/shard_map/ppermute | solution.py:15
  134.7 31.5 %collective-permute-start.4 = (f32[2,5,3,16,1,128]{5,3,2,1,4,0:T(8,128)}, f32[2,5,3,16,1,128]{5,3,2,1,4,0:T(8,128)S(1)}, u32[]{:S(2)}, u32[]{:S(2)}) collective-permute-start(f32[2,5,3,16,1,128]{5,3,2,1,4,0:T(8,128)} %get-tuple-element.29), channel_id=1, source_target_pairs={{4,0},{8,4},{12,8},{16,12},{20,16},{24,20},{28,24},{0,28},{5,1},{9... | collective-permute-start | bytes 737288 | tf_op jit(solution)/shard_map/ppermute | solution.py:18
  166.4 10.1 %copy-start.5 = (f32[5,3,16,8,128]{4,2,1,0,3:T(8,128)S(1)}, f32[5,3,16,8,128]{4,2,1,0,3:T(8,128)}, u32[]{:S(2)}) copy-start(f32[5,3,16,8,128]{4,2,1,0,3:T(8,128)} %get-tuple-element.26) | copy-start | bytes 2949124
  166.4 6.8 %collective-permute-start.6 = (f32[2,5,3,1,10,128]{5,3,2,1,4,0:T(1,128)S(1)}, f32[2,5,3,1,10,128]{5,3,2,1,4,0:T(1,128)S(1)}, u32[]{:S(2)}, u32[]{:S(2)}) collective-permute-start(f32[2,5,3,1,10,128]{5,3,2,1,4,0:T(1,128)S(1)} %get-tuple-element.22), channel_id=1, source_target_pairs={{1,0},{2,1},{3,2},{0,3},{5,4},{6,5},{7,6},{4,7},{9,8},{10,9},{11,1... | collective-permute-start | bytes 460808 | tf_op jit(solution)/shard_map/ppermute | solution.py:18
  166.5 9.6 %collective-permute-start.7 = (f32[2,5,3,1,10,128]{5,3,2,1,4,0:T(1,128)S(1)}, f32[2,5,3,1,10,128]{5,3,2,1,4,0:T(1,128)S(1)}, u32[]{:S(2)}, u32[]{:S(2)}) collective-permute-start(f32[2,5,3,1,10,128]{5,3,2,1,4,0:T(1,128)S(1)} %get-tuple-element.23), channel_id=1, source_target_pairs={{0,1},{1,2},{2,3},{3,0},{4,5},{5,6},{6,7},{7,4},{8,9},{9,10},{10,1... | collective-permute-start | bytes 460808 | tf_op jit(solution)/shard_map/ppermute | solution.py:15
  168.8 8.0 %copy-start.4 = (f32[5,3,16,8,128]{4,3,2,1,0:T(8,128)S(1)}, f32[5,3,16,8,128]{4,3,2,1,0:T(8,128)}, u32[]{:S(2)}) copy-start(f32[5,3,16,8,128]{4,3,2,1,0:T(8,128)} %copy-done.3) | copy-start | bytes 2949124
  168.8 8.0 %copy-start.6 = (f32[1,5,3,16,8,128]{5,4,3,2,1,0:T(8,128)S(1)}, f32[1,5,3,16,8,128]{5,4,3,2,1,0:T(8,128)}, u32[]{:S(2)}) copy-start(f32[1,5,3,16,8,128]{5,4,3,2,1,0:T(8,128)} %copy.252) | copy-start | bytes 2949124
where the time goes:
time: 179 us
  blocking collectives  129 us (72%)
  local copies, waits for them, and re-layouts  11.1 us (6%)
  waiting for transfers between devices  10.7 us (6%)
  starting transfers between devices  10.1 us (6%)
  other arithmetic  9.29 us (5%)
  between operations  4.59 us (3%)
  matrix products  3.63 us (2%)
    psum x4, blocking collectives, broadcast(): return lax.psum(block, axis)  84 us
    all_gather x2, blocking collectives, on_device(): east_whole = lax.all_gather(east_beside, 'ty', axis=2, tiled=True)  26.9 us
    all_gather x2, blocking collectives, on_device(): north_whole = lax.all_gather(north_below, 'tx', axis=2, tiled=True)  18.2 us
    ppermute x4, starting transfers between devices, with_halo(): lax.ppermute(lax.slice_in_dim(block, 0, width, axis=dim), axis, backward)  5.73 us
    ppermute x4, waiting for transfers between devices, with_halo(): lax.ppermute(lax.slice_in_dim(block, block.shape[dim] - width, None, axis...  5.56 us
    ppermute x4, waiting for transfers between devices, with_halo(): lax.ppermute(lax.slice_in_dim(block, 0, width, axis=dim), axis, backward)  5.12 us
    ppermute x4, starting transfers between devices, with_halo(): lax.ppermute(lax.slice_in_dim(block, block.shape[dim] - width, None, axis...  4.4 us
    dot_general x2, matrix products, on_device(): jnp.einsum('slm,skyxl->skyxm', vertical_inverse, adjoint, precision=lax.P...  3.63 us
  transfers between devices with their start and end apart: 8, of which 4 were waited for; matrix products, arithmetic and copies ran while one was open for 5% of the time, Pallas kernels for 0%

commit v1 on v0

--- a/solution.py
+++ b/solution.py
@@ -22,7 +22,12 @@
 
 def broadcast(block, axis, source):
     block = jnp.where(lax.axis_index(axis) == source, block, jnp.zeros_like(block))
-    return lax.psum(block, axis)
+
+    def _obtain_case(frame):
+        x_new = lax.all_gather(frame, axis)
+        return jnp.sum(x_new, axis=0)
+
+    return _obtain_case(block)
 
 
 def link_tables(links, own_tile, tile_count, slot_count):

time: 179 us -> 143 us (0.80)
  blocking collectives: 129 us -> 91.3 us
    psum x4 -> x0, blocking collectives: 84 us -> none  [broadcast(): return lax.psum(block, axis)]
    all_gather x0 -> x4, blocking collectives: none -> 45.2 us  [_obtain_case(): x_new = lax.all_gather(frame, axis)]
    ppermute x4, starting transfers between devices: 5.73 us -> 10.7 us  [with_halo(): lax.ppermute(lax.slice_in_dim(block, 0, width, axis=dim), axis, backward)]
    ppermute x4, starting transfers between devices: 4.4 us -> 1.12 us  [with_halo(): lax.ppermute(lax.slice_in_dim(block, block.shape[dim] - width, None, axis...]
    unnamed x23 -> x27, local copies, waits for them, and re-layouts: 2.87 us -> 3.64 us
  transfers between devices with their start and end apart: 8 -> 8, of which waited for: 4 -> 3; matrix products, arithmetic and copies ran while one was open for 5% -> 6% of each run, Pallas kernels for 0% -> 0%
where the time goes in v1:
time: 143 us; the launch traced here: 142 us
  blocking collectives  91.3 us (64%)
  starting transfers between devices  11.8 us (8%)
  local copies, waits for them, and re-layouts  11.4 us (8%)
  waiting for transfers between devices  10.1 us (7%)
  other arithmetic  9.8 us (7%)
  between operations  4.24 us (3%)
  matrix products  3.63 us (3%)
    all_gather x4, blocking collectives, _obtain_case(): x_new = lax.all_gather(frame, axis)  45.2 us
    all_gather x2, blocking collectives, on_device(): east_whole = lax.all_gather(east_beside, 'ty', axis=2, tiled=True)  27.8 us
    all_gather x2, blocking collectives, on_device(): north_whole = lax.all_gather(north_below, 'tx', axis=2, tiled=True)  18.2 us
    ppermute x4, starting transfers between devices, with_halo(): lax.ppermute(lax.slice_in_dim(block, 0, width, axis=dim), axis, backward)  10.7 us
    ppermute x4, waiting for transfers between devices, with_halo(): lax.ppermute(lax.slice_in_dim(block, block.shape[dim] - width, None, axis...  5.91 us
    ppermute x4, waiting for transfers between devices, with_halo(): lax.ppermute(lax.slice_in_dim(block, 0, width, axis=dim), axis, backward)  4.23 us
    unnamed x27, local copies, waits for them, and re-layouts  3.64 us
    dot_general x2, matrix products, on_device(): jnp.einsum('slm,skyxl->skyxm', vertical_inverse, adjoint, precision=lax.P...  3.63 us
  transfers between devices with their start and end apart: 8, of which 3 were waited for; matrix products, arithmetic and copies ran while one was open for 6% of the time, Pallas kernels for 0%

profile of v1, /device:TPU:0, one launch (start us, length us, event | category | flops | bytes accessed | tf_op | source)
XLA Modules:
  0.0 142.3 jit_solution(10310639860936791499)
XLA Ops:
  0.0 1.2 copy.244
  1.3 1.9 %fusion.13 = f32[5,3,16,8,128]{4,3,2,1,0:T(8,128)S(1)} fusion(f32[5,3,16,8,128]{4,3,2,1,0:T(8,128)S(1)} %copy-done, f32[5,128,128]{2,1,0:T(8,128)} %param.6), kind=kOutput, calls=%fused_computation.33 | convolution fusion | flops 377487360 | bytes 2293760 | tf_op jit(solution)/shard_map/slm,skyxl->skyxm/dot_general | solution.py:80
  3.3 0.9 copy-done.1
  4.6 0.8 fusion.36
  5.9 2.9 %collective-permute-start = (f32[2,5,3,16,1,128]{5,3,2,1,4,0:T(8,128)}, f32[2,5,3,16,1,128]{5,3,2,1,4,0:T(8,128)}, u32[]{:S(2)}, u32[]{:S(2)}) collective-permute-start(f32[2,5,3,16,1,128]{5,3,2,1,4,0:T(8,128)} %get-tuple-element.33), channel_id=1, source_target_pairs={{4,0},{8,4},{12,8},{16,12},{20,16},{24,20},{28,24},{0,28},{5,1},{9... | collective-permute-start | bytes 737288 | tf_op jit(solution)/shard_map/ppermute | solution.py:18
  8.8 0.7 fusion.28
  13.5 14.2 %all-gather = f32[4,5,1,1,8,128]{5,4,3,2,1,0:T(8,128)S(1)} all-gather(f32[1,5,1,1,8,128]{5,4,3,2,1,0:T(8,128)S(1)} %copy.246), channel_id=2, replica_groups=mesh['tx'=8,'ty'=4] {'ty'}, dimensions={0}, use_global_device_ids=true | all-gather | bytes 102400 | tf_op jit(solution)/shard_map/all_gather | solution.py:27
  27.7 9.4 %all-gather.1 = f32[5,64,128]{2,1,0:T(8,128)S(1)} all-gather(f32[5,8,128]{2,1,0:T(8,128)S(1)} %reduce.6), channel_id=3, replica_groups=mesh['tx'=8,'ty'=4] {'tx'}, dimensions={1}, use_global_device_ids=true | all-gather | bytes 184320 | tf_op jit(solution)/shard_map/all_gather | solution.py:92
  37.8 0.8 select_bitcast_fusion.1
  38.6 8.5 %all-gather.2 = f32[8,5,1,16,1,128]{5,3,4,2,1,0:T(8,128)S(1)} all-gather(f32[1,5,1,16,1,128]{5,3,4,2,1,0:T(8,128)S(1)} %select_bitcast_fusion.1), channel_id=4, replica_groups=mesh['tx'=8,'ty'=4] {'tx'}, dimensions={0}, use_global_device_ids=true | all-gather | bytes 368640 | tf_op jit(solution)/shard_map/all_gather | solution.py:27
  47.2 14.3 %all-gather.3 = f32[5,64,128]{2,1,0:T(8,128)} all-gather(f32[5,16,128]{2,1,0:T(8,128)S(1)} %bitcast_reduce_fusion.1), channel_id=5, replica_groups=mesh['tx'=8,'ty'=4] {'ty'}, dimensions={1}, use_global_device_ids=true | all-gather | bytes 204800 | tf_op jit(solution)/shard_map/all_gather | solution.py:94
  61.5 0.7 constant_dynamic-slice_fusion.2
  62.4 1.3 pad_maximum_fusion.13
  63.7 3.8 %collective-permute-start.2 = (f32[2,5,3,1,10,128]{5,3,2,1,4,0:T(1,128)S(1)}, f32[2,5,3,1,10,128]{5,3,2,1,4,0:T(1,128)S(1)}, u32[]{:S(2)}, u32[]{:S(2)}) collective-permute-start(f32[2,5,3,1,10,128]{5,3,2,1,4,0:T(1,128)S(1)} %get-tuple-element.24), channel_id=1, source_target_pairs={{1,0},{2,1},{3,2},{0,3},{5,4},{6,5},{7,6},{4,7},{9,8},{10,9},{11,1... | collective-permute-start | bytes 460808 | tf_op jit(solution)/shard_map/ppermute | solution.py:18
  67.5 0.9 slice_bitcast_fusion.4
  68.4 0.9 slice_bitcast_fusion.5
  69.4 1.0 bitcast_select_fusion.2
  70.4 0.9 bitcast_select_fusion.1
  71.5 2.9 %collective-permute-done.3 = f32[2,5,3,1,10,128]{5,3,2,1,4,0:T(1,128)S(1)} collective-permute-done((f32[2,5,3,1,10,128]{5,3,2,1,4,0:T(1,128)S(1)}, f32[2,5,3,1,10,128]{5,3,2,1,4,0:T(1,128)S(1)}, u32[]{:S(2)}, u32[]{:S(2)}) %collective-permute-start.3) | collective-permute-done | bytes 153632 | tf_op jit(solution)/shard_map/ppermute | solution.py:15
  75.2 1.7 %fusion.9 = f32[5,3,16,8,128]{4,3,2,1,0:T(8,128)S(1)} fusion(f32[5,3,16,8,128]{4,2,1,0,3:T(8,128)S(1)} %fusion.5, f32[5,3,16,8,128]{4,3,2,1,0:T(8,128)S(1)} %copy-done.2, f32[5,3,16,8,128]{4,2,1,0,3:T(8,128)S(1)} %fusion.7, f32[5,128,128]{2,1,0:T(8,128)S(1)} %copy-done.6), kind=kOutput, calls=%fused_computation.23 | convolution fusion | flops 378224640 | bytes 4259840 | tf_op jit(solution)/shard_map/slm,skyxl->skyxm/dot_general | solution.py:80
  78.6 1.4 %slice_bitcast_fusion = (f32[5,3,16,8,128]{4,2,1,0,3:T(8,128)}, f32[1,5,3,16,8,128]{5,3,2,1,4,0:T(8,128)}) fusion(f32[2,5,3,16,8,128]{5,3,2,1,4,0:T(8,128)S(1)} %broadcast_multiply_fusion), kind=kLoop, calls=%fused_computation.3 | loop fusion | bytes 3932160 | tf_op jit(solution)/shard_map/squeeze | solution.py:109
  80.1 13.2 %all-gather.4 = f32[4,5,1,1,8,128]{5,4,3,2,1,0:T(8,128)S(1)} all-gather(f32[1,5,1,1,8,128]{5,4,3,2,1,0:T(8,128)S(1)} %copy.265), channel_id=6, replica_groups=mesh['tx'=8,'ty'=4] {'ty'}, dimensions={0}, use_global_device_ids=true | all-gather | bytes 102400 | tf_op jit(solution)/shard_map/all_gather | solution.py:27
  93.3 0.8 select_bitcast_fusion
  94.1 9.3 %all-gather.6 = f32[8,5,1,16,1,128]{5,3,4,2,1,0:T(8,128)S(1)} all-gather(f32[1,5,1,16,1,128]{5,3,4,2,1,0:T(8,128)S(1)} %select_bitcast_fusion), channel_id=8, replica_groups=mesh['tx'=8,'ty'=4] {'tx'}, dimensions={0}, use_global_device_ids=true | all-gather | bytes 368640 | tf_op jit(solution)/shard_map/all_gather | solution.py:27
  103.5 13.5 %all-gather.7 = f32[5,64,128]{2,1,0:T(8,128)S(1)} all-gather(f32[5,16,128]{2,1,0:T(8,128)S(1)} %bitcast_reduce_fusion), channel_id=9, replica_groups=mesh['tx'=8,'ty'=4] {'ty'}, dimensions={1}, use_global_device_ids=true | all-gather | bytes 204800 | tf_op jit(solution)/shard_map/all_gather | solution.py:94
  117.0 2.6 %collective-permute-start.4 = (f32[2,5,3,16,1,128]{5,3,2,1,4,0:T(8,128)S(1)}, f32[2,5,3,16,1,128]{5,3,2,1,4,0:T(8,128)S(1)}, u32[]{:S(2)}, u32[]{:S(2)}) collective-permute-start(f32[2,5,3,16,1,128]{5,3,2,1,4,0:T(8,128)S(1)} %get-tuple-element.29), channel_id=1, source_target_pairs={{4,0},{8,4},{12,8},{16,12},{20,16},{24,20},{28,24},{0,28},{5,1},{9... | collective-permute-start | bytes 737288 | tf_op jit(solution)/shard_map/ppermute | solution.py:18
  119.6 1.5 %copy.318 = f32[1,5,3,16,8,128]{5,4,3,2,1,0:T(8,128)S(1)} copy(f32[1,5,3,16,8,128]{5,3,2,1,4,0:T(8,128)} %get-tuple-element.27) | data formatting | bytes 1966080 | tf_op jit(solution)/shard_map/slice | solution.py:106
  121.2 8.8 %all-gather.5 = f32[5,64,128]{2,1,0:T(8,128)S(1)} all-gather(f32[5,8,128]{2,1,0:T(8,128)S(1)} %reduce.8), channel_id=7, replica_groups=mesh['tx'=8,'ty'=4] {'tx'}, dimensions={1}, use_global_device_ids=true | all-gather | bytes 184320 | tf_op jit(solution)/shard_map/all_gather | solution.py:92
  130.2 1.4 collective-permute-start.6
  132.6 4.2 %collective-permute-done.6 = f32[2,5,3,1,10,128]{5,3,2,1,4,0:T(1,128)S(1)} collective-permute-done((f32[2,5,3,1,10,128]{5,3,2,1,4,0:T(1,128)S(1)}, f32[2,5,3,1,10,128]{5,3,2,1,4,0:T(1,128)S(1)}, u32[]{:S(2)}, u32[]{:S(2)}) %collective-permute-start.6) | collective-permute-done | bytes 153632 | tf_op jit(solution)/shard_map/ppermute | solution.py:18
  136.9 3.0 %collective-permute-done.7 = f32[2,5,3,1,10,128]{5,3,2,1,4,0:T(1,128)S(1)} collective-permute-done((f32[2,5,3,1,10,128]{5,3,2,1,4,0:T(1,128)S(1)}, f32[2,5,3,1,10,128]{5,3,2,1,4,0:T(1,128)S(1)}, u32[]{:S(2)}, u32[]{:S(2)}) %collective-permute-start.7) | collective-permute-done | bytes 153632 | tf_op jit(solution)/shard_map/ppermute | solution.py:15
  140.6 1.8 %fusion.4 = f32[5,3,16,8,128]{4,3,2,1,0:T(8,128)} fusion(f32[5,3,16,8,128]{4,3,2,1,0:T(8,128)S(1)} %copy-done.4, f32[5,3,16,8,128]{4,3,2,1,0:T(8,128)S(1)} %bitcast.129, f32[5,3,16,1,128]{4,3,2,1,0:T(1,128)S(1)} %bitcast.139, f32[5,3,16,1,128]{4,3,2,1,0:T(1,128)S(1)} %bitcast.138, f32[5,3,16,8,128]{4,2,1,0,3:T(8,128)S(1)} %fusion), kind=kLoop, calls=%fused_computation.8 | loop fusion | flops 1720320 | bytes 4177920 | tf_op jit(solution)/shard_map/add | solution.py:112
  (84 shorter events, 6.6 us)
Async XLA Ops:
  0.0 1.3 copy-start
  3.3 0.9 copy-start.1
  4.4 4.3 %copy-start.7 = (s32[40,4]{0,1:T(4,128)S(1)}, s32[40,4]{0,1:T(4,128)}, u32[]{:S(2)}) copy-start(s32[40,4]{0,1:T(4,128)} %param.7) | copy-start | bytes 1924
  5.4 57.0 %collective-permute-start.1 = (f32[2,5,3,16,1,128]{5,3,2,1,4,0:T(8,128)}, f32[2,5,3,16,1,128]{5,3,2,1,4,0:T(8,128)}, u32[]{:S(2)}, u32[]{:S(2)}) collective-permute-start(f32[2,5,3,16,1,128]{5,3,2,1,4,0:T(8,128)} %get-tuple-element.32), channel_id=1, source_target_pairs={{0,4},{4,8},{8,12},{12,16},{16,20},{20,24},{24,28},{28,0},{1,5},{5... | collective-permute-start | bytes 737288 | tf_op jit(solution)/shard_map/ppermute | solution.py:15
  5.9 56.5 %collective-permute-start = (f32[2,5,3,16,1,128]{5,3,2,1,4,0:T(8,128)}, f32[2,5,3,16,1,128]{5,3,2,1,4,0:T(8,128)}, u32[]{:S(2)}, u32[]{:S(2)}) collective-permute-start(f32[2,5,3,16,1,128]{5,3,2,1,4,0:T(8,128)} %get-tuple-element.33), channel_id=1, source_target_pairs={{4,0},{8,4},{12,8},{16,12},{20,16},{24,20},{28,24},{0,28},{5,1},{9... | collective-permute-start | bytes 737288 | tf_op jit(solution)/shard_map/ppermute | solution.py:18
  12.9 56.5 %copy-start.8 = (f32[3]{0:T(128)}, f32[3]{0:T(128)S(1)}, u32[]{:S(2)}) copy-start(f32[3]{0:T(128)S(1)} %neg.18) | copy-start | bytes 40
  63.7 7.8 %collective-permute-start.2 = (f32[2,5,3,1,10,128]{5,3,2,1,4,0:T(1,128)S(1)}, f32[2,5,3,1,10,128]{5,3,2,1,4,0:T(1,128)S(1)}, u32[]{:S(2)}, u32[]{:S(2)}) collective-permute-start(f32[2,5,3,1,10,128]{5,3,2,1,4,0:T(1,128)S(1)} %get-tuple-element.24), channel_id=1, source_target_pairs={{1,0},{2,1},{3,2},{0,3},{5,4},{6,5},{7,6},{4,7},{9,8},{10,9},{11,1... | collective-permute-start | bytes 460808 | tf_op jit(solution)/shard_map/ppermute | solution.py:18
  67.5 7.0 %collective-permute-start.3 = (f32[2,5,3,1,10,128]{5,3,2,1,4,0:T(1,128)S(1)}, f32[2,5,3,1,10,128]{5,3,2,1,4,0:T(1,128)S(1)}, u32[]{:S(2)}, u32[]{:S(2)}) collective-permute-start(f32[2,5,3,1,10,128]{5,3,2,1,4,0:T(1,128)S(1)} %get-tuple-element.25), channel_id=1, source_target_pairs={{0,1},{1,2},{2,3},{3,0},{4,5},{5,6},{6,7},{7,4},{8,9},{9,10},{10,1... | collective-permute-start | bytes 460808 | tf_op jit(solution)/shard_map/ppermute | solution.py:15
  71.4 3.7 %copy-start.2 = (f32[5,3,16,8,128]{4,3,2,1,0:T(8,128)S(1)}, f32[5,3,16,8,128]{4,3,2,1,0:T(8,128)}, u32[]{:S(2)}) copy-start(f32[5,3,16,8,128]{4,3,2,1,0:T(8,128)} %copy-done.1) | copy-start | bytes 2949124
  71.5 3.7 %copy-start.6 = (f32[5,128,128]{2,1,0:T(8,128)S(1)}, f32[5,128,128]{2,1,0:T(8,128)}, u32[]{:S(2)}) copy-start(f32[5,128,128]{2,1,0:T(8,128)} %param.6) | copy-start | bytes 983044
  76.9 0.9 copy-start.3
  117.0 13.0 %collective-permute-start.5 = (f32[2,5,3,16,1,128]{5,3,2,1,4,0:T(8,128)S(1)}, f32[2,5,3,16,1,128]{5,3,2,1,4,0:T(8,128)S(1)}, u32[]{:S(2)}, u32[]{:S(2)}) collective-permute-start(f32[2,5,3,16,1,128]{5,3,2,1,4,0:T(8,128)S(1)} %get-tuple-element.28), channel_id=1, source_target_pairs={{0,4},{4,8},{8,12},{12,16},{16,20},{20,24},{24,28},{28,0},{1,5},{5... | collective-permute-start | bytes 737288 | tf_op jit(solution)/shard_map/ppermute | solution.py:15
  117.0 13.0 %collective-permute-start.4 = (f32[2,5,3,16,1,128]{5,3,2,1,4,0:T(8,128)S(1)}, f32[2,5,3,16,1,128]{5,3,2,1,4,0:T(8,128)S(1)}, u32[]{:S(2)}, u32[]{:S(2)}) collective-permute-start(f32[2,5,3,16,1,128]{5,3,2,1,4,0:T(8,128)S(1)} %get-tuple-element.29), channel_id=1, source_target_pairs={{4,0},{8,4},{12,8},{16,12},{20,16},{24,20},{28,24},{0,28},{5,1},{9... | collective-permute-start | bytes 737288 | tf_op jit(solution)/shard_map/ppermute | solution.py:18
  130.0 2.5 %copy-start.9 = (f32[3]{0:T(128)S(1)}, f32[3]{0:T(128)}, u32[]{:S(2)}) copy-start(f32[3]{0:T(128)} %copy-done.8) | copy-start | bytes 40
  130.2 10.1 %copy-start.5 = (f32[5,3,16,8,128]{4,2,1,0,3:T(8,128)S(1)}, f32[5,3,16,8,128]{4,2,1,0,3:T(8,128)}, u32[]{:S(2)}) copy-start(f32[5,3,16,8,128]{4,2,1,0,3:T(8,128)} %get-tuple-element.26) | copy-start | bytes 2949124
  130.2 6.6 %collective-permute-start.6 = (f32[2,5,3,1,10,128]{5,3,2,1,4,0:T(1,128)S(1)}, f32[2,5,3,1,10,128]{5,3,2,1,4,0:T(1,128)S(1)}, u32[]{:S(2)}, u32[]{:S(2)}) collective-permute-start(f32[2,5,3,1,10,128]{5,3,2,1,4,0:T(1,128)S(1)} %get-tuple-element.22), channel_id=1, source_target_pairs={{1,0},{2,1},{3,2},{0,3},{5,4},{6,5},{7,6},{4,7},{9,8},{10,9},{11,1... | collective-permute-start | bytes 460808 | tf_op jit(solution)/shard_map/ppermute | solution.py:18
  131.6 8.2 %collective-permute-start.7 = (f32[2,5,3,1,10,128]{5,3,2,1,4,0:T(1,128)S(1)}, f32[2,5,3,1,10,128]{5,3,2,1,4,0:T(1,128)S(1)}, u32[]{:S(2)}, u32[]{:S(2)}) collective-permute-start(f32[2,5,3,1,10,128]{5,3,2,1,4,0:T(1,128)S(1)} %get-tuple-element.23), channel_id=1, source_target_pairs={{0,1},{1,2},{2,3},{3,0},{4,5},{5,6},{6,7},{7,4},{8,9},{9,10},{10,1... | collective-permute-start | bytes 460808 | tf_op jit(solution)/shard_map/ppermute | solution.py:15
  132.5 8.0 %copy-start.4 = (f32[5,3,16,8,128]{4,3,2,1,0:T(8,128)S(1)}, f32[5,3,16,8,128]{4,3,2,1,0:T(8,128)}, u32[]{:S(2)}) copy-start(f32[5,3,16,8,128]{4,3,2,1,0:T(8,128)} %copy-done.3) | copy-start | bytes 2949124
